TPU v7x, 512 devices: a whole 4x4x16 slice. The times are simulated.
512 devices in a mesh: basis: 2 (over z_hi), eig: 32 (over y, z_lo), chan: 8 (over x, core).
Axes of the slice: x: 4, y: 4, z: 16 (z_hi: 2, z_lo: 8; z = z_hi * 8 + z_lo), core: 2. Of those that a mesh axis runs over, the one named last changes fastest.
Arguments:
- eigvecs: bfloat16 [2048, 5120], P('eig', 'basis'), may hold values from -6 to 6
- boundary: bfloat16 [5120, 4096], P('basis', 'chan'), may hold values from -0.3125 to 0.3125
- block_sizes: int32 [16], replicated, may hold values from 256 to 768, as said below
- target_of_channel: int32 [4096], P('chan'), may hold values from 0 to 15, as said below
- poles: float32 [2048], replicated, may hold values from -4 to 4, as said below
- energies: float32 [16], P('basis'), may hold values from -0.25 to 0.25
Outputs:
- rmatrix: float32 [16, 4096, 4096], P('basis', 'chan', 'eig')
Inputs may be any that keep to these rules, and one draw needn't show every extreme that they name: `poles`: every pole lies 0.5 or more away from zero, with both signs present. `block_sizes`: the sizes sum to 5120; every target state's block holds at least 256 basis rows. `target_of_channel`: every target state has exactly 256 channels.
All inputs are finite; a program needn't handle non-finite values.
Results may differ from a plain program's by a relative error of at most 0.0049.
Values may be sent and summed in bfloat16 or wider, within the bound.
A program may use at most 128 MiB of HBM per device.

v0:
```python
import jax
import jax.numpy as jnp
from jax import lax
from jax.sharding import PartitionSpec as P


def per_device(eigvecs, boundary, block_sizes, target_of_channel, poles, energies):
    rows_here = eigvecs.shape[1]
    block_ends = jnp.cumsum(block_sizes)
    row_ids = lax.axis_index("basis") * rows_here + jnp.arange(rows_here, dtype=jnp.int32)
    owner_of = jnp.sum((block_ends[None, :] <= row_ids[:, None]).astype(jnp.int32), axis=1)
    member = owner_of[:, None] == target_of_channel[None, :]
    masked = jnp.where(member, boundary, jnp.zeros_like(boundary))
    partial_value = jnp.dot(eigvecs, masked, preferred_element_type=jnp.float32)
    amplitudes = lax.psum(partial_value, "basis").astype(jnp.bfloat16)
    all_channels = lax.all_gather(amplitudes, "chan", axis=1, tiled=True)
    own_width = amplitudes.shape[1]
    own_first = lax.axis_index("chan") * own_width
    col_width = all_channels.shape[1] // lax.axis_size("eig")
    col_first = lax.axis_index("eig") * col_width
    factor = poles.shape[0] ** (-0.5)
    weights = 1.0 / (poles[None, :] - energies[:, None])
    panel_in = lax.all_gather(all_channels, "eig", axis=0, tiled=True)
    left_panel = lax.dynamic_slice_in_dim(panel_in, own_first, own_width, 1)
    right_panel = lax.dynamic_slice_in_dim(panel_in, col_first, col_width, 1)
    scaled = (weights[:, :, None] * left_panel[None].astype(jnp.float32)).astype(jnp.bfloat16)
    summed = jnp.einsum("ekc,kd->ecd", scaled, right_panel, preferred_element_type=jnp.float32)
    return summed * factor


def solution(mesh):
    placed = (P("eig", "basis"), P("basis", "chan"), P(), P("chan"), P(), P("basis"))
    return jax.shard_map(
        per_device, mesh=mesh, in_specs=placed, out_specs=P("basis", "chan", "eig"), check_vma=False
    )
```

profile of v0, /device:TPU:1, one launch (start us, length us, event | category | flops | bytes accessed | tf_op | source)
XLA Modules:
  0.0 461.5 jit_solution(13660114059671404453)
XLA Ops:
  6.5 0.0 copy-start
  6.5 0.0 copy-start.1
  6.5 0.0 copy-start.2
  6.5 0.0 all-gather.2.cloned.1.call-start
  6.6 0.8 copy.11
  7.4 0.1 reduce
  7.5 0.1 convert_reduce_fusion
  7.6 0.0 copy-done
  7.6 2.9 fusion.8
  10.5 29.8 %all-reduce.1 = bf16[64,512]{1,0:T(8,128)(2,1)S(1)} all-reduce(f32[64,512]{1,0:T(8,128)S(1)} %fusion.8), channel_id=1, replica_groups=mesh['basis'=2,'eig'=32,'chan'=8] {'basis'}, use_global_device_ids=true, to_apply=%region_2.3 | all-reduce | flops 32768 | bytes 196608 | tf_op jit(solution)/shard_map/psum | solution.py:15
  40.3 22.0 %all_gather.6 = bf16[64,4096]{1,0:T(8,128)(2,1)} all-gather(bf16[64,512]{1,0:T(8,128)(2,1)S(1)} %all-reduce.1), channel_id=1, replica_groups=mesh['basis'=2,'eig'=32,'chan'=8] {'chan'}, dimensions={1}, use_global_device_ids=true | all-gather | bytes 589824 | tf_op jit(solution)/shard_map/all_gather | solution.py:16
  62.3 0.0 all-gather.2.cloned.1.call-update
  62.4 0.0 copy-done.1
  62.4 0.0 copy-done.2
  62.4 0.1 subtract_divide_fusion
  62.5 374.4 %all-gather.2.cloned.1.call-done = bf16[2048,4096]{1,0:T(8,128)(2,1)} async-done(((bf16[64,4096]{1,0:T(8,128)(2,1)}), bf16[2048,4096]{1,0:T(8,128)(2,1)}) %all-gather.2.cloned.1.call-update) | async-done | bytes 16777232 | tf_op jit(solution)/shard_map/all_gather | solution.py:23
  436.9 4.2 dynamic-slice_convert_fusion
  441.1 5.4 %copy.12 = f32[2048,512]{0,1:T(8,128)} copy(f32[2048,512]{1,0:T(8,128)} %dynamic-slice_convert_fusion) | data formatting | bytes 8388608 | tf_op jit(solution)/shard_map/convert_element_type | solution.py:26
  446.4 8.2 %fusion.6 = f32[8,512,128]{2,1,0:T(8,128)} fusion(f32[2048,512]{0,1:T(8,128)} %copy.12, f32[8,2048]{1,0:T(8,128)S(1)} %subtract_divide_fusion, bf16[2048,4096]{1,0:T(8,128)(2,1)} %all-gather.2.cloned.1.call-done, s32[]{:T(128)S(6)} %select_n.12), kind=kOutput, calls=%fused_computation.9 | convolution fusion | flops 2164785152 | bytes 6881284 | tf_op jit(solution)/shard_map/ekc,kd->ecd/dot_general | solution.py:27
  (2 shorter events, 0.0 us)
Async XLA Ops:
  6.5 1.1 copy-start
  6.5 55.8 %copy-start.1 = (f32[2048]{0:T(1024)S(1)}, f32[2048]{0:T(1024)}, u32[]{:S(2)}) copy-start(f32[2048]{0:T(1024)} %param.10) | copy-start | bytes 24580
  6.5 55.8 %copy-start.2 = (f32[8]{0:T(128)S(1)}, f32[8]{0:T(128)}, u32[]{:S(2)}) copy-start(f32[8]{0:T(128)} %param.11) | copy-start | bytes 100
  6.5 430.4 %all-gather.2.cloned.1.call-start = ((), (), s32[]{:S(2)}) async-start(), calls=%async_computation | async-start | bytes 17301504 | tf_op jit(solution)/shard_map/all_gather | solution.py:23
Sparse Core Ops, SparseCore 0:
  62.5 374.3 all-gather.1
where the time goes:
time: 462 us; the launch traced here: 461 us
  waiting for transfers between devices  374 us (81%)
  blocking collectives  51.8 us (11%)
  between operations  13.5 us (3%)
  matrix products  11 us (2%)
  local copies, waits for them, and re-layouts  6.16 us (1%)
    all_gather x1, waiting for transfers between devices, per_device(): panel_in = lax.all_gather(all_channels, 'eig', axis=0, tiled=True)  374 us
    psum x1, blocking collectives, per_device(): amplitudes = lax.psum(partial_value, 'basis').astype(jnp.bfloat16)  29.8 us
    all_gather x1, blocking collectives, per_device(): all_channels = lax.all_gather(amplitudes, 'chan', axis=1, tiled=True)  22 us
  transfers between devices with their start and end apart: 1, of which 1 were waited for; matrix products, arithmetic and copies ran while one was open for 0% of the time, Pallas kernels for 0%

commit v1 on v0

v1 whole, which is shorter than its diff:
```python
import jax
import jax.numpy as jnp
from jax import lax
from jax.experimental import pallas as pl
from jax.experimental.pallas import tpu as pltpu
from jax.sharding import PartitionSpec as P

MESH = pl.DeviceIdType.MESH
NY, NZL, NX = 4, 8, 4
NS = 2


def remote(src, dst, send, recv, where):
    return pltpu.make_async_remote_copy(
        src_ref=src, dst_ref=dst, send_sem=send, recv_sem=recv, device_id=where, device_id_type=MESH
    )


def kernel(
    eig_hbm, bnd_hbm, sizes, tgt, poles, energies, out,
    eig, bnd, part, psend, precv, G, D, wrow, wcol, LT, BS,
    eig_sem, bnd_sem, xs, xr, zs, zr, ys, yr, fs, fr, ds, dr,
):
    h, e, c = lax.axis_index("basis"), lax.axis_index("eig"), lax.axis_index("chan")
    y, zl = e // NZL, e % NZL
    x, core = c // 2, c % 2
    z = h * NZL + zl
    rows = bnd.shape[1]

    def at_z(zz):
        return (zz // NZL, y * NZL + zz % NZL, c)

    across = (1 - h, e, c)
    zplus, zminus = at_z((z + 1) % 16), at_z((z + 15) % 16)
    yplus = (h, ((y + 1) % NY) * NZL + zl, c)
    yminus = (h, ((y + 3) % NY) * NZL + zl, c)
    xplus = (h, e, ((x + 1) % NX) * 2 + core)
    xminus = (h, e, ((x + 3) % NX) * 2 + core)
    twin = (h, e, x * 2 + (1 - core))

    barrier = pltpu.get_barrier_semaphore()
    for who in (across, zplus, zminus, yplus, yminus, xplus, xminus, twin):
        pl.semaphore_signal(barrier, inc=1, device_id=who, device_id_type=MESH)

    eig_copy = pltpu.make_async_copy(eig_hbm, eig, eig_sem)
    eig_copy.start()

    def bnd_copy(b):
        return pltpu.make_async_copy(
            bnd_hbm.at[:, pl.ds(pl.multiple_of(b * 128, 128), 128)], bnd.at[b], bnd_sem.at[b]
        )

    for b in range(4):
        bnd_copy(b).start()
    eig_copy.wait()

    @pl.loop(0, 4)
    def _(b):
        bnd_copy(b).wait()
        t = tgt[pl.ds(b, 1), :]
        lo = jnp.zeros((1, 128), jnp.int32)
        hi = jnp.zeros((1, 128), jnp.int32)
        for k in range(16):
            lo = lo + jnp.where(t > k, sizes[k], 0)
            hi = hi + jnp.where(t >= k, sizes[k], 0)
        lo = lo - h * rows
        hi = hi - h * rows
        step = rows // 5
        total = jnp.zeros((64, 128), jnp.float32)
        for i in range(5):
            row = lax.broadcasted_iota(jnp.int32, (step, 128), 0) + i * step
            keep = jnp.logical_and(row >= lo, row < hi)
            vals = bnd[b, i * step : (i + 1) * step, :].astype(jnp.float32)
            masked = jnp.where(keep, vals, 0.0).astype(jnp.bfloat16)
            total = total + jnp.dot(
                eig[:, i * step : (i + 1) * step], masked, preferred_element_type=jnp.float32
            )
        part[b] = total
        psend[b] = total.astype(jnp.bfloat16)

    pl.semaphore_wait(barrier, 8)

    def cross(b):
        return remote(psend.at[b], precv.at[b], xs.at[b], xr.at[b], across)

    for b in range(4):
        cross(b).start()

    for k in range(8):
        wrow[k] = (wrow.shape[1] * 128) ** -0.5 / (poles[...] - energies[k])
    for i in range(16):
        turned = jnp.transpose(wrow[:, i, :])
        wcol[i // 4, (i % 4) * 2 : (i % 4) * 2 + 2] = turned.reshape(2, 64, 8)

    @pl.loop(0, 8)
    def _(k):
        out[k] = jnp.zeros(out.shape[1:], jnp.float32)

    def at(q):
        return (zl + ((q + 1) // 2) * (1 - 2 * (q % 2)) + NZL) % NZL

    def shard(s, yy, q):
        return G.at[pl.ds(s * (4 // NS), 4 // NS), yy, at(q)]

    def z_copy(s, up, q, nxt):
        return remote(
            shard(s, y, q), shard(s, y, q), zs.at[s, up, q], zr.at[s, nxt], zplus if up else zminus
        )

    def y_copy(s, up, q):
        return remote(
            shard(s, y, q), shard(s, y, q), ys.at[s, up, q], yr.at[s, up, q], yplus if up else yminus
        )

    def f_copy(s, up, q):
        yy = (y + (3 if up else 1)) % NY
        return remote(shard(s, yy, q), shard(s, yy, q), fs.at[s, q], fr.at[s, q], yplus if up else yminus)

    def d_copy(k, q):
        to = (twin, xplus, xminus)[k]
        return remote(D.at[:, at(q)], D.at[:, at(q)], ds.at[k, q], dr.at[q], to)

    kap = zl // 4
    r = (x - y + NX) % NX
    mine = core == kap
    origin = jnp.logical_and(mine, r == 0)

    def d_local(q):
        return pltpu.make_async_copy(G.at[zl % 4, :, at(q)], D.at[:, at(q)], dr.at[q])

    def sends_up(q):
        return jnp.logical_and(mine, jnp.logical_or(r == 0, jnp.logical_and(r == 1, q % 2 == 0)))

    def sends_down(q):
        return jnp.logical_and(mine, jnp.logical_or(r == 0, jnp.logical_and(r == 3, q % 2 == 1)))

    def z_up_from(q):
        return jnp.logical_or(q == 0, jnp.logical_and(q % 2 == 1, q + 2 < 8 - core))

    def z_down_from(q):
        return jnp.logical_and(q % 2 == 0, q + 2 < 8 + core)

    def do_z(s, q):
        @pl.when(q > 0)
        def _():
            z_copy(s, 1, q, q).wait_recv()

        @pl.when(z_up_from(q))
        def _():
            z_copy(s, 1, q, q + 1 + (q + 7) // 8).start()

        @pl.when(z_down_from(q))
        def _():
            z_copy(s, 0, q, q + 2 - q // 6).start()

    def do_y(s, q):
        y_copy(s, 1, q).start()
        y_copy(s, 0, q).start()

    def do_f(s, q):
        y_copy(s, 1, q).wait_recv()
        y_copy(s, 0, q).wait_recv()

        @pl.when(core == 0)
        def _():
            f_copy(s, 1, q).start()

        @pl.when(core == 1)
        def _():
            f_copy(s, 0, q).start()

    def do_d0(q):
        for s in range(NS):
            f_copy(s, 1, q).wait_recv()

        @pl.when(origin)
        def _():
            d_local(q).start()

    def do_d1(q):
        @pl.when(origin)
        def _():
            d_local(q).wait()

        @pl.when(jnp.logical_not(origin))
        def _():
            d_copy(0, q).wait_recv()

        @pl.when(mine)
        def _():
            d_copy(0, q).start()

        @pl.when(sends_up(q))
        def _():
            d_copy(1, q).start()

        @pl.when(sends_down(q))
        def _():
            d_copy(2, q).start()

    def do_mm(q):
        p = at(q)
        for b in range(4):
            LT[b * 128 : (b + 1) * 128, :] = jnp.transpose(G[b, :, p].reshape(256, 128))
        dv = D[:, p].reshape(256, 128).astype(jnp.float32)
        w = wcol[:, p].reshape(256, 8)
        for k in range(8):
            BS[k // 2, :, (k % 2) * 128 : (k % 2 + 1) * 128] = (w[:, k : k + 1] * dv).astype(jnp.bfloat16)

        @pl.loop(0, 4)
        def _(n):
            got = jnp.dot(LT[...], BS[n], preferred_element_type=jnp.float32)
            out[2 * n] += got[:, :128]
            out[2 * n + 1] += got[:, 128:]

    for b in range(4):
        cross(b).wait_recv()
        G[b, y, zl] = (part[b] + precv[b].astype(jnp.float32)).astype(jnp.bfloat16)

    LAG = 5

    @pl.loop(0, 8 + LAG)
    def _(q):
        @pl.when(q < 8)
        def _():
            for s in range(NS):
                do_z(s, q)
                do_y(s, q)

        @pl.when(jnp.logical_and(q >= 1, q < 9))
        def _():
            for s in range(NS):
                do_f(s, q - 1)

        @pl.when(jnp.logical_and(q >= 2, q < 10))
        def _():
            do_d0(q - 2)

        @pl.when(jnp.logical_and(q >= 3, q < 11))
        def _():
            do_d1(q - 3)

        @pl.when(q >= LAG)
        def _():
            do_mm(q - LAG)

    for b in range(4):
        cross(b).wait_send()

    @pl.loop(0, 8)
    def _(q):
        for s in range(NS):
            @pl.when(z_up_from(q))
            def _():
                z_copy(s, 1, q, q).wait_send()

            @pl.when(z_down_from(q))
            def _():
                z_copy(s, 0, q, q).wait_send()

            y_copy(s, 1, q).wait_send()
            y_copy(s, 0, q).wait_send()
            f_copy(s, 1, q).wait_send()

        @pl.when(mine)
        def _():
            d_copy(0, q).wait_send()

        @pl.when(sends_up(q))
        def _():
            d_copy(1, q).wait_send()

        @pl.when(sends_down(q))
        def _():
            d_copy(2, q).wait_send()


def per_device(eigvecs, boundary, block_sizes, target_of_channel, poles, energies):
    rows = boundary.shape[0]
    vm, sm, anyw = (
        pl.BlockSpec(memory_space=pltpu.VMEM), pl.BlockSpec(memory_space=pltpu.SMEM), pl.BlockSpec(memory_space=pl.ANY)
    )
    bf, f32, dma = jnp.bfloat16, jnp.float32, pltpu.SemaphoreType.DMA
    return pl.pallas_call(
        kernel,
        out_shape=jax.ShapeDtypeStruct((8, 512, 128), f32),
        in_specs=[anyw, anyw, sm, vm, vm, sm],
        out_specs=vm,
        scratch_shapes=[
            pltpu.VMEM((64, rows), bf),
            pltpu.VMEM((4, rows, 128), bf),
            pltpu.VMEM((4, 64, 128), f32),
            pltpu.VMEM((4, 64, 128), bf),
            pltpu.VMEM((4, 64, 128), bf),
            pltpu.VMEM((4, NY, NZL, 64, 128), bf),
            pltpu.VMEM((NY, NZL, 64, 128), bf),
            pltpu.VMEM((8, 16, 128), f32),
            pltpu.VMEM((NY, NZL, 64, 8), f32),
            pltpu.VMEM((512, 256), bf),
            pltpu.VMEM((4, 256, 256), bf),
            dma, dma((4,)), dma((4,)), dma((4,)),
            dma((NS, 2, 8)), dma((NS, 8)),
            dma((NS, 2, 8)), dma((NS, 2, 8)),
            dma((NS, 8)), dma((NS, 8)),
            dma((3, 8)), dma((8,)),
        ],
        compiler_params=pltpu.CompilerParams(
            collective_id=0, has_side_effects=True, vmem_limit_bytes=40 * 2**20
        ),
        cost_estimate=pl.CostEstimate(flops=2_400_000_000, bytes_accessed=5_000_000, transcendentals=0),
    )(eigvecs, boundary, block_sizes, target_of_channel.reshape(4, 128), poles.reshape(16, 128), energies)


def solution(mesh):
    placed = (P("eig", "basis"), P("basis", "chan"), P(), P("chan"), P(), P("basis"))
    return jax.shard_map(
        per_device, mesh=mesh, in_specs=placed, out_specs=P("basis", "chan", "eig"), check_vma=False
    )
```

time: 462 us -> 89.3 us (0.19)
  the two profiles are of different devices: /device:TPU:1 before, /device:TPU:27 now
where the time goes in v1:
time: 89.3 us; the launch traced here: 89 us
  Pallas kernels  82.3 us (92%)
  local copies, waits for them, and re-layouts  6.72 us (8%)
    pallas_call x1, Pallas kernels, per_device(): pl.pallas_call(kernel, out_shape=jax.ShapeDtypeStruct((8, 512, 128), f32)...  82.3 us
    unnamed x13, local copies, waits for them, and re-layouts  6.72 us

profile of v1, /device:TPU:27, one launch (start us, length us, event | category | flops | bytes accessed | tf_op | source)
XLA Modules:
  0.0 89.0 jit_solution(15152575587505126312)
XLA Ops:
  0.0 0.0 copy-start
  0.0 1.7 %copy-done = bf16[2560,512]{1,0:T(8,128)(2,1)S(1)} copy-done((bf16[2560,512]{1,0:T(8,128)(2,1)S(1)}, bf16[2560,512]{1,0:T(8,128)(2,1)}, u32[]{:S(2)}) %copy-start) | copy-done | bytes 2621464
  1.7 0.0 copy-start.1
  1.7 1.0 %copy-done.1 = bf16[64,2560]{1,0:T(8,128)(2,1)S(1)} copy-done((bf16[64,2560]{1,0:T(8,128)(2,1)S(1)}, bf16[64,2560]{1,0:T(8,128)(2,1)}, u32[]{:S(2)}) %copy-start.1) | copy-done | bytes 327704
  2.7 0.0 copy-start.2
  2.7 0.7 copy-done.2
  3.4 0.0 copy-start.3
  3.4 0.7 copy-done.3
  4.1 0.0 copy-start.4
  4.1 0.7 copy-done.4
  4.7 0.0 copy-start.5
  4.8 0.7 copy-done.5
  5.4 82.3 %shard_map.64 = f32[8,512,128]{2,1,0:T(8,128)S(1)} custom-call(bf16[64,2560]{1,0:T(8,128)(2,1)S(1)} %copy-done.1, bf16[2560,512]{1,0:T(8,128)(2,1)S(1)} %copy-done, s32[16]{0:T(128)S(1)} %copy-done.4, s32[4,128]{1,0:T(4,128)S(1)} %bitcast.3, f32[16,128]{1,0:T(8,128)S(1)} %bitcast.2, f32[8]{0:T(128)S(1)} %copy-done.5), custom_call_target="tpu_custom_call" | custom-call | flops 2400000000 | bytes 5000000 | tf_op jit(solution)/shard_map/pallas_call | solution.py:284
  87.7 1.3 %copy.8 = f32[8,512,128]{2,1,0:T(8,128)} copy(f32[8,512,128]{2,1,0:T(8,128)S(1)} %shard_map.64) | data formatting | bytes 4194304
Async XLA Ops:
  0.0 1.7 %copy-start = (bf16[2560,512]{1,0:T(8,128)(2,1)S(1)}, bf16[2560,512]{1,0:T(8,128)(2,1)}, u32[]{:S(2)}) copy-start(bf16[2560,512]{1,0:T(8,128)(2,1)} %bnd_hbm.1) | copy-start | bytes 7864324
  1.7 1.0 %copy-start.1 = (bf16[64,2560]{1,0:T(8,128)(2,1)S(1)}, bf16[64,2560]{1,0:T(8,128)(2,1)}, u32[]{:S(2)}) copy-start(bf16[64,2560]{1,0:T(8,128)(2,1)} %eig_hbm.1) | copy-start | bytes 983044
  2.7 0.7 copy-start.2
  3.4 0.7 copy-start.3
  4.1 0.7 copy-start.4
  4.7 0.7 copy-start.5

commit v2 on v0

v2 whole, which is shorter than its diff:
```python
import jax
import jax.numpy as jnp
from jax import lax
from jax.experimental import pallas as pl
from jax.experimental.pallas import tpu as pltpu
from jax.sharding import PartitionSpec as P

MESH = pl.DeviceIdType.MESH
NY, NZL, NX, NZ = 4, 8, 4, 16
NS = 2
LAGS = (3, 6, 10, 12, 20)


def remote(src, dst, send, recv, where):
    return pltpu.make_async_remote_copy(
        src_ref=src, dst_ref=dst, send_sem=send, recv_sem=recv, device_id=where, device_id_type=MESH
    )


def kernel(
    eig_hbm, bnd_hbm, sizes_hbm, tgt_hbm, poles_hbm, energies_hbm, out,
    sizes, tgt, poles, energies, small_sem, eig, bnd, psend, precv, G, D, wrow, wcol, LT, BS,
    eig_sem, bnd_sem, xs, xr, zs, zf, zr, ys, yr, fs, fr, ds, dr,
):
    h, e, c = lax.axis_index("basis"), lax.axis_index("eig"), lax.axis_index("chan")
    y, zl = e // NZL, e % NZL
    x, core = c // 2, c % 2
    z = h * NZL + zl
    rows = bnd.shape[1]

    def at_z(far):
        zz = (z + far + NZ) % NZ
        return (zz // NZL, y * NZL + zz % NZL, c)

    y_to = [(h, ((y + k) % NY) * NZL + zl, c) for k in (1, 3)]
    x_to = [(h, e, ((x + k) % NX) * 2 + core) for k in (1, 3, 2)]
    twin = (h, e, x * 2 + (1 - core))
    partners = [at_z(k) for k in (4, -4, 1, -1, 2, -2)] + y_to + x_to + [twin]

    barrier = pltpu.get_barrier_semaphore()
    for who in partners:
        pl.semaphore_signal(barrier, inc=1, device_id=who, device_id_type=MESH)

    small = [
        pltpu.make_async_copy(src, dst, small_sem.at[i])
        for i, (src, dst) in enumerate(
            ((sizes_hbm, sizes), (tgt_hbm, tgt), (poles_hbm, poles), (energies_hbm, energies))
        )
    ]
    eig_copy = pltpu.make_async_copy(eig_hbm, eig, eig_sem)

    def bnd_copy(s):
        return pltpu.make_async_copy(bnd_hbm.at[:, s * 256 : (s + 1) * 256], bnd.at[s], bnd_sem.at[s])

    for copy in small:
        copy.start()
    eig_copy.start()
    for s in range(NS):
        bnd_copy(s).start()
    for copy in small:
        copy.wait()
    eig_copy.wait()

    def cross(s):
        down = (s - h) * (s - h)
        return remote(psend.at[s], precv.at[down], xs.at[s], xr.at[down], at_z(4 - 8 * down))

    step = rows // 5
    for s in range(NS):
        bnd_copy(s).wait()
        t = jnp.concatenate([tgt[2 * s : 2 * s + 1, :], tgt[2 * s + 1 : 2 * s + 2, :]], axis=1)
        lo = jnp.zeros((1, 256), jnp.int32)
        hi = jnp.zeros((1, 256), jnp.int32)
        for k in range(16):
            lo = lo + jnp.where(t > k, sizes[k], 0)
            hi = hi + jnp.where(t >= k, sizes[k], 0)
        lo = lo - h * rows
        hi = hi - h * rows
        total = jnp.zeros((64, 256), jnp.float32)
        for i in range(5):
            row = lax.broadcasted_iota(jnp.int32, (step, 256), 0) + i * step
            keep = jnp.logical_and(row >= lo, row < hi)
            vals = bnd[s, i * step : (i + 1) * step, :].astype(jnp.float32)
            masked = jnp.where(keep, vals, 0.0).astype(jnp.bfloat16)
            total = total + jnp.dot(
                eig[:, i * step : (i + 1) * step], masked, preferred_element_type=jnp.float32
            )
        for j in range(2):
            psend[s, j] = total[:, j * 128 : (j + 1) * 128].astype(jnp.bfloat16)
        if s == 0:
            pl.semaphore_wait(barrier, len(partners))
        cross(s).start()

    for k in range(8):
        wrow[k] = (wrow.shape[1] * 128) ** -0.5 / (poles[...] - energies[k])
    for i in range(16):
        turned = jnp.transpose(wrow[:, i, :])
        wcol[i // 4, (i % 4) * 2 : (i % 4) * 2 + 2] = turned.reshape(2, 64, 8)

    @pl.loop(0, 8)
    def _(k):
        out[k] = jnp.zeros(out.shape[1:], jnp.float32)

    def shard(q, yy):
        m = (z + ((q + 1) // 2) * (1 - 2 * (q % 2)) + NZ) % NZ
        return G.at[((m + 12) % NZ) // NZL, :, yy, (m + 4) % NZL]

    def z_own(k):
        far, q = ((2, 3), (-2, 4), (1, 1), (-1, 2))[k]
        return remote(shard(0, y), shard(0, y), zs.at[k], zr.at[q], at_z(far))

    def z_up(q):
        return remote(shard(q, y), shard(q, y), zf.at[q], zr.at[q + 4], at_z(2))

    def z_down(q):
        return remote(shard(q, y), shard(q, y), zf.at[q], zr.at[q + 4 - q // 12], at_z(-2))

    def goes_up(q):
        return jnp.logical_and(q % 2 == 1, q + core < 12)

    def goes_down(q):
        return jnp.logical_and(jnp.logical_and(q % 2 == 0, q > 0), q < 12 + core)

    def y_copy(k, q):
        return remote(shard(q, y), shard(q, y), ys.at[k, q], yr.at[k, q], y_to[k])

    def f_copy(q):
        yy = (y + 3 - 2 * core) % NY
        to = (h, ((y + 1 + 2 * core) % NY) * NZL + zl, c)
        return remote(shard(q, yy), shard(q, yy), fs.at[q], fr.at[q], to)

    def at(q):
        return (zl + ((q + 1) // 2) * (1 - 2 * (q % 2)) + 20) % NZL

    def needed(q):
        m = (z + ((q + 1) // 2) * (1 - 2 * (q % 2)) + NZ) % NZ
        return ((m + 12) % NZ) // NZL == (zl % 4) // 2

    kap = zl // 4
    r = (x - y + NX) % NX
    mine = core == kap
    origin = jnp.logical_and(mine, r == 0)
    relay = jnp.logical_and(mine, r != 0)

    def d_copy(k, q):
        p = at(q)
        return remote(G.at[(zl % 4) // 2, zl % 2, :, p], D.at[:, p], ds.at[k, q], dr.at[q], (x_to + [twin])[k])

    def d_twin(q):
        p = at(q)
        return remote(D.at[:, p], D.at[:, p], ds.at[3, q], dr.at[q], twin)

    def d_local(q):
        p = at(q)
        return pltpu.make_async_copy(G.at[(zl % 4) // 2, zl % 2, :, p], D.at[:, p], dr.at[q])

    cross(0).wait_recv()
    cross(1).wait_recv()
    for j in range(2):
        both = precv[0, j].astype(jnp.float32) + precv[1, j].astype(jnp.float32)
        G[((z + 12) % NZ) // NZL, j, y, (zl + 4) % NZL] = both.astype(jnp.bfloat16)
    for k in range(4):
        z_own(k).start()

    def do_z(q):
        @pl.when(q > 0)
        def _():
            remote(shard(q, y), shard(q, y), zf.at[q], zr.at[q], at_z(1)).wait_recv()

        @pl.when(goes_up(q))
        def _():
            z_up(q).start()

        @pl.when(goes_down(q))
        def _():
            z_down(q).start()

        for k in range(2):
            y_copy(k, q).start()

    def do_f(q):
        for k in range(2):
            y_copy(k, q).wait_recv()
        f_copy(q).start()

    def do_d0(q):
        f_copy(q).wait_recv()

        @pl.when(jnp.logical_and(origin, needed(q)))
        def _():
            for k in (2, 0, 1, 3):
                d_copy(k, q).start()
            d_local(q).start()

    def do_d1(q):
        @pl.when(jnp.logical_and(origin, needed(q)))
        def _():
            d_local(q).wait()

        @pl.when(jnp.logical_and(relay, needed(q)))
        def _():
            d_twin(q).wait_recv()
            d_twin(q).start()

    def do_d2(q):
        @pl.when(jnp.logical_and(jnp.logical_not(mine), needed(q)))
        def _():
            d_twin(q).wait_recv()

    def do_mm(i):
        p = (zl + 12 + ((8 - i) // 2) * (2 * (i % 2) - 1)) % NZL
        for b in range(4):
            LT[b * 128 : (b + 1) * 128, :] = jnp.transpose(G[b // 2, b % 2, :, p].reshape(256, 128))
        dv = D[:, p].reshape(256, 128).astype(jnp.float32)
        w = wcol[:, p].reshape(256, 8)
        for k in range(8):
            BS[k // 2, :, (k % 2) * 128 : (k % 2 + 1) * 128] = (w[:, k : k + 1] * dv).astype(jnp.bfloat16)

        @pl.loop(0, 4)
        def _(n):
            got = jnp.dot(LT[...], BS[n], preferred_element_type=jnp.float32)
            out[2 * n] += got[:, :128]
            out[2 * n + 1] += got[:, 128:]

    def during(t, lag, count, do):
        @pl.when(jnp.logical_and(t >= lag, t < lag + count))
        def _():
            do(t - lag)

    @pl.loop(0, LAGS[-1] + 8)
    def _(t):
        during(t, 0, 16, do_z)
        during(t, LAGS[0], 16, do_f)
        during(t, LAGS[1], 16, do_d0)
        during(t, LAGS[2], 16, do_d1)
        during(t, LAGS[3], 16, do_d2)
        during(t, LAGS[4], 8, do_mm)

    for s in range(NS):
        cross(s).wait_send()
    for k in range(4):
        z_own(k).wait_send()

    @pl.loop(0, 16)
    def _(q):
        @pl.when(jnp.logical_or(goes_up(q), goes_down(q)))
        def _():
            z_up(q).wait_send()

        for k in range(2):
            y_copy(k, q).wait_send()
        f_copy(q).wait_send()

        @pl.when(jnp.logical_and(origin, needed(q)))
        def _():
            for k in range(4):
                d_copy(k, q).wait_send()

        @pl.when(jnp.logical_and(relay, needed(q)))
        def _():
            d_twin(q).wait_send()


def per_device(eigvecs, boundary, block_sizes, target_of_channel, poles, energies):
    rows = boundary.shape[0]
    bf, f32, dma = jnp.bfloat16, jnp.float32, pltpu.SemaphoreType.DMA
    given = (eigvecs, boundary, block_sizes, target_of_channel.reshape(4, 128), poles.reshape(16, 128), energies)
    return pl.pallas_call(
        kernel,
        out_shape=jax.ShapeDtypeStruct((8, 512, 128), f32),
        in_specs=[pl.BlockSpec(memory_space=pl.ANY)] * 6,
        out_specs=pl.BlockSpec(memory_space=pltpu.VMEM),
        scratch_shapes=[
            pltpu.SMEM((16,), jnp.int32),
            pltpu.VMEM((4, 128), jnp.int32),
            pltpu.VMEM((16, 128), f32),
            pltpu.SMEM((8,), f32),
            dma((4,)),
            pltpu.VMEM((64, rows), bf),
            pltpu.VMEM((NS, rows, 256), bf),
            pltpu.VMEM((2, 2, 64, 128), bf),
            pltpu.VMEM((2, 2, 64, 128), bf),
            pltpu.VMEM((2, 2, NY, NZL, 64, 128), bf),
            pltpu.VMEM((NY, NZL, 64, 128), bf),
            pltpu.VMEM((8, 16, 128), f32),
            pltpu.VMEM((NY, NZL, 64, 8), f32),
            pltpu.VMEM((512, 256), bf),
            pltpu.VMEM((4, 256, 256), bf),
            dma, dma((NS,)), dma((NS,)), dma((NS,)),
            dma((4,)), dma((16,)), dma((16,)),
            dma((2, 16)), dma((2, 16)),
            dma((16,)), dma((16,)),
            dma((4, 16)), dma((16,)),
        ],
        compiler_params=pltpu.CompilerParams(
            collective_id=0, has_side_effects=True, vmem_limit_bytes=42 * 2**20
        ),
        cost_estimate=pl.CostEstimate(flops=2_400_000_000, bytes_accessed=5_000_000, transcendentals=0),
    )(*(pltpu.with_memory_space_constraint(a, pltpu.HBM) for a in given))


def solution(mesh):
    placed = (P("eig", "basis"), P("basis", "chan"), P(), P("chan"), P(), P("basis"))
    return jax.shard_map(
        per_device, mesh=mesh, in_specs=placed, out_specs=P("basis", "chan", "eig"), check_vma=False
    )
```

time: 462 us -> 61 us (0.13)
  the two profiles are of different devices: /device:TPU:1 before, /device:TPU:32 now
where the time goes in v2:
time: 61 us; the launch traced here: 60.8 us
  Pallas kernels  59.5 us (98%)
  local copies, waits for them, and re-layouts  1.32 us (2%)
    pallas_call x1, Pallas kernels, per_device(): pl.pallas_call(kernel, out_shape=jax.ShapeDtypeStruct((8, 512, 128), f32)...  59.5 us
    unnamed x1, local copies, waits for them, and re-layouts  1.32 us

profile of v2, /device:TPU:32, one launch (start us, length us, event | category | flops | bytes accessed | tf_op | source)
XLA Modules:
  0.0 60.8 jit_solution(17910464185623407340)
XLA Ops:
  0.0 59.5 %shard_map.64 = f32[8,512,128]{2,1,0:T(8,128)S(1)} custom-call(bf16[64,2560]{1,0:T(8,128)(2,1)} %eig_hbm.1, bf16[2560,512]{1,0:T(8,128)(2,1)} %bnd_hbm.1, s32[16]{0:T(128)} %sizes_hbm.1, s32[4,128]{1,0:T(4,128)} %bitcast.3, f32[16,128]{1,0:T(8,128)} %bitcast.2, f32[8]{0:T(128)} %energies_hbm.1), custom_call_target="tpu_custom_call" | custom-call | flops 2400000000 | bytes 5000000 | tf_op jit(solution)/shard_map/pallas_call | solution.py:268
  59.5 1.3 %copy.8 = f32[8,512,128]{2,1,0:T(8,128)} copy(f32[8,512,128]{2,1,0:T(8,128)S(1)} %shard_map.64) | data formatting | bytes 4194304

commit v3 on v2

v3 whole, which is shorter than its diff:
```python
import jax
import jax.numpy as jnp
from jax import lax
from jax.experimental import pallas as pl
from jax.experimental.pallas import tpu as pltpu
from jax.sharding import PartitionSpec as P

MESH = pl.DeviceIdType.MESH
NY, NZL, NX, NZ = 4, 8, 4, 16
NS = 2
LAGS = (3, 5, 8, 9, 9)


def remote(src, dst, send, recv, where):
    return pltpu.make_async_remote_copy(
        src_ref=src, dst_ref=dst, send_sem=send, recv_sem=recv, device_id=where, device_id_type=MESH
    )


def kernel(
    eig_hbm, bnd_hbm, sizes_hbm, tgt_hbm, poles_hbm, energies_hbm, out,
    sizes, tgt, poles, energies, small_sem, eig, bnd, psend, precv, G, D, wrow, wcol, wide, LT, BS,
    eig_sem, bnd_sem, xs, xr, zs, zf, zr, ys, yr, fs, fr, ds, dr,
):
    h, e, c = lax.axis_index("basis"), lax.axis_index("eig"), lax.axis_index("chan")
    y, zl = e // NZL, e % NZL
    x, core = c // 2, c % 2
    z = h * NZL + zl
    rows = bnd.shape[0]

    def at_z(far):
        zz = (z + far + NZ) % NZ
        return (zz // NZL, y * NZL + zz % NZL, c)

    y_to = [(h, ((y + k) % NY) * NZL + zl, c) for k in (1, 3)]
    x_to = [(h, e, ((x + k) % NX) * 2 + core) for k in (1, 3, 2)]
    twin = (h, e, x * 2 + (1 - core))
    partners = [at_z(k) for k in (4, -4, 1, -1, 2, -2)] + y_to + x_to + [twin]

    barrier = pltpu.get_barrier_semaphore()
    for who in partners:
        pl.semaphore_signal(barrier, inc=1, device_id=who, device_id_type=MESH)

    small = [
        pltpu.make_async_copy(src, dst, small_sem.at[i])
        for i, (src, dst) in enumerate(
            ((sizes_hbm, sizes), (tgt_hbm, tgt), (poles_hbm, poles), (energies_hbm, energies))
        )
    ]
    eig_copy = pltpu.make_async_copy(eig_hbm, eig, eig_sem)

    step = rows // 5

    def bnd_copy(i):
        part = pl.ds(i * step, step)
        return pltpu.make_async_copy(bnd_hbm.at[part], bnd.at[part], bnd_sem.at[i])

    for copy in small:
        copy.start()
    eig_copy.start()
    for i in range(5):
        bnd_copy(i).start()
    for copy in small:
        copy.wait()

    def cross(s, down):
        return remote(psend.at[s], precv.at[down, s], xs.at[s, down], xr.at[s, down], at_z(4 - 8 * down))

    t = jnp.concatenate([tgt[b : b + 1, :] for b in range(4)], axis=1)
    lo = jnp.zeros((1, 512), jnp.int32)
    hi = jnp.zeros((1, 512), jnp.int32)
    for k in range(16):
        lo = lo + jnp.where(t > k, sizes[k], 0)
        hi = hi + jnp.where(t >= k, sizes[k], 0)
    lo = lo - h * rows
    hi = hi - h * rows
    eig_copy.wait()
    total = jnp.zeros((64, 512), jnp.float32)
    for i in range(5):
        bnd_copy(i).wait()
        row = lax.broadcasted_iota(jnp.int32, (step, 512), 0) + i * step
        keep = jnp.logical_and(row >= lo, row < hi)
        vals = bnd[i * step : (i + 1) * step, :].astype(jnp.float32)
        masked = jnp.where(keep, vals, 0.0).astype(jnp.bfloat16)
        total = total + jnp.dot(
            eig[:, i * step : (i + 1) * step], masked, preferred_element_type=jnp.float32
        )
    for b in range(4):
        psend[b // 2, b % 2] = total[:, b * 128 : (b + 1) * 128].astype(jnp.bfloat16)
    pl.semaphore_wait(barrier, len(partners))
    for s in range(NS):
        for down in range(2):
            cross(s, down).start()

    for k in range(8):
        wrow[k] = (wrow.shape[1] * 128) ** -0.5 / (poles[...] - energies[k])
    for i in range(16):
        wcol[i] = jnp.transpose(wrow[:, i, :])

    @pl.loop(0, 16)
    def _(i):
        for k in range(8):
            across = jnp.broadcast_to(wcol[i, :, k : k + 1], (128, 128))
            wide[k, i // 4, pl.ds((i % 4) * 2, 2)] = across.reshape(2, 64, 128)

    @pl.loop(0, 8)
    def _(k):
        out[k] = jnp.zeros(out.shape[1:], jnp.float32)

    def at(q):
        return (zl + ((q + 1) // 2) * (1 - 2 * (q % 2)) + 12) % NZL

    def shard(s, q, yy):
        return G.at[s, :, yy, at(q)]

    def z_own(s, k):
        far, q = ((2, 3), (-2, 4), (1, 1), (-1, 2))[k]
        return remote(shard(s, 0, y), shard(s, 0, y), zs.at[s, k], zr.at[s, q], at_z(far))

    def z_up(s, q):
        return remote(shard(s, q, y), shard(s, q, y), zf.at[s, q], zr.at[s, q + 4], at_z(2))

    def z_down(s, q):
        return remote(shard(s, q, y), shard(s, q, y), zf.at[s, q], zr.at[s, q + 4 - q // 4], at_z(-2))

    def goes_up(q):
        return jnp.logical_and(q % 2 == 1, q + core < 4)

    def goes_down(q):
        return jnp.logical_and(jnp.logical_and(q % 2 == 0, q > 0), q < 4 + core)

    def y_copy(s, k, q):
        return remote(shard(s, q, y), shard(s, q, y), ys.at[s, k, q], yr.at[s, k, q], y_to[k])

    def f_copy(s, q):
        yy = (y + 3 - 2 * core) % NY
        to = (h, ((y + 1 + 2 * core) % NY) * NZL + zl, c)
        return remote(shard(s, q, yy), shard(s, q, yy), fs.at[s, q], fr.at[s, q], to)

    kap = zl // 4
    r = (x - y + NX) % NX
    mine = core == kap
    origin = jnp.logical_and(mine, r == 0)
    relay = jnp.logical_and(mine, r != 0)

    def d_copy(k, q):
        p = at(q)
        return remote(G.at[(zl % 4) // 2, zl % 2, :, p], D.at[:, p], ds.at[k, q], dr.at[q], (x_to + [twin])[k])

    def d_twin(q):
        p = at(q)
        return remote(D.at[:, p], D.at[:, p], ds.at[3, q], dr.at[q], twin)

    def d_local(q):
        p = at(q)
        return pltpu.make_async_copy(G.at[(zl % 4) // 2, zl % 2, :, p], D.at[:, p], dr.at[q])

    for s in range(NS):
        for down in range(2):
            cross(s, down).wait_recv()
        for j in range(2):
            both = precv[0, s, j].astype(jnp.float32) + precv[1, s, j].astype(jnp.float32)
            G[s, j, y, (zl + 4) % NZL] = both.astype(jnp.bfloat16)
        for k in range(4):
            z_own(s, k).start()

    def do_z(q):
        for s in range(NS):
            @pl.when(q > 0)
            def _():
                remote(shard(s, q, y), shard(s, q, y), zf.at[s, q], zr.at[s, q], at_z(1)).wait_recv()

            @pl.when(goes_up(q))
            def _():
                z_up(s, q).start()

            @pl.when(goes_down(q))
            def _():
                z_down(s, q).start()

            for k in range(2):
                y_copy(s, k, q).start()

    def do_f(q):
        for s in range(NS):
            for k in range(2):
                y_copy(s, k, q).wait_recv()
            f_copy(s, q).start()

    def do_d0(q):
        for s in range(NS):
            f_copy(s, q).wait_recv()

        @pl.when(origin)
        def _():
            for k in (2, 0, 1, 3):
                d_copy(k, q).start()
            d_local(q).start()

    def do_d1(q):
        @pl.when(origin)
        def _():
            d_local(q).wait()

        @pl.when(relay)
        def _():
            d_twin(q).wait_recv()
            d_twin(q).start()

    def do_d2(q):
        @pl.when(jnp.logical_not(mine))
        def _():
            d_twin(q).wait_recv()

    def do_mm(q):
        p = at(q)
        for b in range(4):
            LT[b * 128 : (b + 1) * 128, :] = jnp.transpose(G[b // 2, b % 2, :, p].reshape(256, 128))
        dv = D[:, p].reshape(256, 128).astype(jnp.float32)
        for k in range(8):
            w = wide[k, :, p].reshape(256, 128)
            BS[k // 2, :, (k % 2) * 128 : (k % 2 + 1) * 128] = (w * dv).astype(jnp.bfloat16)
        for n in range(4):
            got = jnp.dot(LT[...], BS[n], preferred_element_type=jnp.float32)
            out[2 * n] += got[:, :128]
            out[2 * n + 1] += got[:, 128:]

    def during(t, lag, count, do):
        @pl.when(jnp.logical_and(t >= lag, t < lag + count))
        def _():
            do(t - lag)

    @pl.loop(0, LAGS[-1] + 8)
    def _(t):
        during(t, 0, 8, do_z)
        during(t, LAGS[0], 8, do_f)
        during(t, LAGS[1], 8, do_d0)
        during(t, LAGS[2], 8, do_d1)
        during(t, LAGS[3], 8, do_d2)
        during(t, LAGS[4], 8, do_mm)

    for s in range(NS):
        for down in range(2):
            cross(s, down).wait_send()
        for k in range(4):
            z_own(s, k).wait_send()

    @pl.loop(0, 8)
    def _(q):
        for s in range(NS):
            @pl.when(jnp.logical_or(goes_up(q), goes_down(q)))
            def _():
                z_up(s, q).wait_send()

            for k in range(2):
                y_copy(s, k, q).wait_send()
            f_copy(s, q).wait_send()

        @pl.when(origin)
        def _():
            for k in range(4):
                d_copy(k, q).wait_send()

        @pl.when(relay)
        def _():
            d_twin(q).wait_send()


def per_device(eigvecs, boundary, block_sizes, target_of_channel, poles, energies):
    rows = boundary.shape[0]
    bf, f32, dma = jnp.bfloat16, jnp.float32, pltpu.SemaphoreType.DMA
    given = (eigvecs, boundary, block_sizes, target_of_channel.reshape(4, 128), poles.reshape(16, 128), energies)
    return pl.pallas_call(
        kernel,
        out_shape=jax.ShapeDtypeStruct((8, 512, 128), f32),
        in_specs=[pl.BlockSpec(memory_space=pl.ANY)] * 6,
        out_specs=pl.BlockSpec(memory_space=pltpu.VMEM),
        scratch_shapes=[
            pltpu.SMEM((16,), jnp.int32),
            pltpu.VMEM((4, 128), jnp.int32),
            pltpu.VMEM((16, 128), f32),
            pltpu.SMEM((8,), f32),
            dma((4,)),
            pltpu.VMEM((64, rows), bf),
            pltpu.VMEM((rows, 512), bf),
            pltpu.VMEM((NS, 2, 64, 128), bf),
            pltpu.VMEM((2, NS, 2, 64, 128), bf),
            pltpu.VMEM((2, 2, NY, NZL, 64, 128), bf),
            pltpu.VMEM((NY, NZL, 64, 128), bf),
            pltpu.VMEM((8, 16, 128), f32),
            pltpu.VMEM((16, 128, 8), f32),
            pltpu.VMEM((8, NY, NZL, 64, 128), f32),
            pltpu.VMEM((512, 256), bf),
            pltpu.VMEM((4, 256, 256), bf),
            dma, dma((5,)), dma((NS, 2)), dma((NS, 2)),
            dma((NS, 4)), dma((NS, 8)), dma((NS, 8)),
            dma((NS, 2, 8)), dma((NS, 2, 8)),
            dma((NS, 8)), dma((NS, 8)),
            dma((4, 8)), dma((8,)),
        ],
        compiler_params=pltpu.CompilerParams(
            collective_id=0, has_side_effects=True, vmem_limit_bytes=42 * 2**20
        ),
        cost_estimate=pl.CostEstimate(flops=2_400_000_000, bytes_accessed=5_000_000, transcendentals=0),
    )(*(pltpu.with_memory_space_constraint(a, pltpu.HBM) for a in given))


def solution(mesh):
    placed = (P("eig", "basis"), P("basis", "chan"), P(), P("chan"), P(), P("basis"))
    return jax.shard_map(
        per_device, mesh=mesh, in_specs=placed, out_specs=P("basis", "chan", "eig"), check_vma=False
    )
```

time: 61 us -> 53.6 us (0.88)
  the two profiles are of different devices: /device:TPU:32 before, /device:TPU:3 now
where the time goes in v3:
time: 53.6 us; the launch traced here: 53.5 us
  Pallas kernels  52.2 us (97%)
  local copies, waits for them, and re-layouts  1.32 us (2%)
    pallas_call x1, Pallas kernels, per_device(): pl.pallas_call(kernel, out_shape=jax.ShapeDtypeStruct((8, 512, 128), f32)...  52.2 us
    unnamed x1, local copies, waits for them, and re-layouts  1.32 us

profile of v3, /device:TPU:3, one launch (start us, length us, event | category | flops | bytes accessed | tf_op | source)
XLA Modules:
  0.0 53.5 jit_solution(17268429644139468324)
XLA Ops:
  0.0 52.2 %shard_map.64 = f32[8,512,128]{2,1,0:T(8,128)S(1)} custom-call(bf16[64,2560]{1,0:T(8,128)(2,1)} %eig_hbm.1, bf16[2560,512]{1,0:T(8,128)(2,1)} %bnd_hbm.1, s32[16]{0:T(128)} %sizes_hbm.1, s32[4,128]{1,0:T(4,128)} %bitcast.3, f32[16,128]{1,0:T(8,128)} %bitcast.2, f32[8]{0:T(128)} %energies_hbm.1), custom_call_target="tpu_custom_call" | custom-call | flops 2400000000 | bytes 5000000 | tf_op jit(solution)/shard_map/pallas_call | solution.py:273
  52.2 1.3 %copy.8 = f32[8,512,128]{2,1,0:T(8,128)} copy(f32[8,512,128]{2,1,0:T(8,128)S(1)} %shard_map.64) | data formatting | bytes 4194304

commit v4 on v3

--- a/solution.py
+++ b/solution.py
@@ -114,7 +114,7 @@
         return G.at[s, :, yy, at(q)]
 
     def z_own(s, k):
-        far, q = ((2, 3), (-2, 4), (1, 1), (-1, 2))[k]
+        far, q = ((1, 1), (-1, 2), (2, 3), (-2, 4))[k]
         return remote(shard(s, 0, y), shard(s, 0, y), zs.at[s, k], zr.at[s, q], at_z(far))
 
     def z_up(s, q):
@@ -161,14 +161,18 @@
         for j in range(2):
             both = precv[0, s, j].astype(jnp.float32) + precv[1, s, j].astype(jnp.float32)
             G[s, j, y, (zl + 4) % NZL] = both.astype(jnp.bfloat16)
-        for k in range(4):
+        for k in range(2):
+            z_own(s, k).start()
+            y_copy(s, k, 0).start()
+        for k in range(2, 4):
             z_own(s, k).start()
 
     def do_z(q):
         for s in range(NS):
-            @pl.when(q > 0)
-            def _():
-                remote(shard(s, q, y), shard(s, q, y), zf.at[s, q], zr.at[s, q], at_z(1)).wait_recv()
+            remote(shard(s, q, y), shard(s, q, y), zf.at[s, q], zr.at[s, q], at_z(1)).wait_recv()
+
+            for k in range(2):
+                y_copy(s, k, q).start()
 
             @pl.when(goes_up(q))
             def _():
@@ -177,9 +181,6 @@
             @pl.when(goes_down(q))
             def _():
                 z_down(s, q).start()
-
-            for k in range(2):
-                y_copy(s, k, q).start()
 
     def do_f(q):
         for s in range(NS):
@@ -232,7 +233,10 @@
 
     @pl.loop(0, LAGS[-1] + 8)
     def _(t):
-        during(t, 0, 8, do_z)
+        @pl.when(jnp.logical_and(t >= 1, t < 8))
+        def _():
+            do_z(t)
+
         during(t, LAGS[0], 8, do_f)
         during(t, LAGS[1], 8, do_d0)
         during(t, LAGS[2], 8, do_d1)

time: 53.6 us -> 52.8 us (0.985)
  Pallas kernels: 52.2 us -> 51.3 us
    pallas_call x1, Pallas kernels: 52.2 us -> 51.3 us  [per_device(): pl.pallas_call(kernel, out_shape=jax.ShapeDtypeStruct((8, 512, 128), f32)...]
where the time goes in v4:
time: 52.8 us; the launch traced here: 52.6 us
  Pallas kernels  51.3 us (97%)
  local copies, waits for them, and re-layouts  1.32 us (2%)
    pallas_call x1, Pallas kernels, per_device(): pl.pallas_call(kernel, out_shape=jax.ShapeDtypeStruct((8, 512, 128), f32)...  51.3 us
    unnamed x1, local copies, waits for them, and re-layouts  1.32 us

profile of v4, /device:TPU:3, one launch (start us, length us, event | category | flops | bytes accessed | tf_op | source)
XLA Modules:
  0.0 52.6 jit_solution(1358848092818413753)
XLA Ops:
  0.0 51.3 %shard_map.64 = f32[8,512,128]{2,1,0:T(8,128)S(1)} custom-call(bf16[64,2560]{1,0:T(8,128)(2,1)} %eig_hbm.1, bf16[2560,512]{1,0:T(8,128)(2,1)} %bnd_hbm.1, s32[16]{0:T(128)} %sizes_hbm.1, s32[4,128]{1,0:T(4,128)} %bitcast.3, f32[16,128]{1,0:T(8,128)} %bitcast.2, f32[8]{0:T(128)} %energies_hbm.1), custom_call_target="tpu_custom_call" | custom-call | flops 2400000000 | bytes 5000000 | tf_op jit(solution)/shard_map/pallas_call | solution.py:277
  51.3 1.3 %copy.8 = f32[8,512,128]{2,1,0:T(8,128)} copy(f32[8,512,128]{2,1,0:T(8,128)S(1)} %shard_map.64) | data formatting | bytes 4194304

commit v5 on v4

--- a/solution.py
+++ b/solution.py
@@ -138,6 +138,8 @@
         return remote(shard(s, q, yy), shard(s, q, yy), fs.at[s, q], fr.at[s, q], to)
 
     kap = zl // 4
+    first = (zl % 4) // 2
+    order = (first, 1 - first)
     r = (x - y + NX) % NX
     mine = core == kap
     origin = jnp.logical_and(mine, r == 0)
@@ -168,7 +170,7 @@
             z_own(s, k).start()
 
     def do_z(q):
-        for s in range(NS):
+        for s in order:
             remote(shard(s, q, y), shard(s, q, y), zf.at[s, q], zr.at[s, q], at_z(1)).wait_recv()
 
             for k in range(2):
@@ -183,14 +185,13 @@
                 z_down(s, q).start()
 
     def do_f(q):
-        for s in range(NS):
+        for s in order:
             for k in range(2):
                 y_copy(s, k, q).wait_recv()
             f_copy(s, q).start()
 
     def do_d0(q):
-        for s in range(NS):
-            f_copy(s, q).wait_recv()
+        f_copy(first, q).wait_recv()
 
         @pl.when(origin)
         def _():
@@ -199,6 +200,8 @@
             d_local(q).start()
 
     def do_d1(q):
+        f_copy(1 - first, q).wait_recv()
+
         @pl.when(origin)
         def _():
             d_local(q).wait()

time: 52.8 us -> 52.9 us (level)
  no operation moved by 1% of the time
where the time goes in v5:
time: 52.9 us; the launch traced here: 52.8 us
  Pallas kernels  51.4 us (97%)
  local copies, waits for them, and re-layouts  1.32 us (2%)
    pallas_call x1, Pallas kernels, per_device(): pl.pallas_call(kernel, out_shape=jax.ShapeDtypeStruct((8, 512, 128), f32)...  51.4 us
    unnamed x1, local copies, waits for them, and re-layouts  1.32 us

profile of v5, /device:TPU:3, one launch (start us, length us, event | category | flops | bytes accessed | tf_op | source)
XLA Modules:
  0.0 52.8 jit_solution(3108537437729991541)
XLA Ops:
  0.0 51.4 %shard_map.64 = f32[8,512,128]{2,1,0:T(8,128)S(1)} custom-call(bf16[64,2560]{1,0:T(8,128)(2,1)} %eig_hbm.1, bf16[2560,512]{1,0:T(8,128)(2,1)} %bnd_hbm.1, s32[16]{0:T(128)} %sizes_hbm.1, s32[4,128]{1,0:T(4,128)} %bitcast.3, f32[16,128]{1,0:T(8,128)} %bitcast.2, f32[8]{0:T(128)} %energies_hbm.1), custom_call_target="tpu_custom_call" | custom-call | flops 2400000000 | bytes 5000000 | tf_op jit(solution)/shard_map/pallas_call | solution.py:280
  51.4 1.3 %copy.8 = f32[8,512,128]{2,1,0:T(8,128)} copy(f32[8,512,128]{2,1,0:T(8,128)S(1)} %shard_map.64) | data formatting | bytes 4194304

commit v6 on v4

--- a/solution.py
+++ b/solution.py
@@ -8,7 +8,7 @@
 MESH = pl.DeviceIdType.MESH
 NY, NZL, NX, NZ = 4, 8, 4, 16
 NS = 2
-LAGS = (3, 5, 8, 9, 9)
+LAGS = (3, 6, 9, 10, 10)
 
 
 def remote(src, dst, send, recv, where):

time: 52.8 us -> 52.5 us (level)
  no operation moved by 1% of the time
where the time goes in v6:
time: 52.5 us; the launch traced here: 52.3 us
  Pallas kernels  51 us (97%)
  local copies, waits for them, and re-layouts  1.32 us (3%)
    pallas_call x1, Pallas kernels, per_device(): pl.pallas_call(kernel, out_shape=jax.ShapeDtypeStruct((8, 512, 128), f32)...  51 us
    unnamed x1, local copies, waits for them, and re-layouts  1.32 us

profile of v6, /device:TPU:3, one launch (start us, length us, event | category | flops | bytes accessed | tf_op | source)
XLA Modules:
  0.0 52.3 jit_solution(13912013218338150512)
XLA Ops:
  0.0 51.0 %shard_map.64 = f32[8,512,128]{2,1,0:T(8,128)S(1)} custom-call(bf16[64,2560]{1,0:T(8,128)(2,1)} %eig_hbm.1, bf16[2560,512]{1,0:T(8,128)(2,1)} %bnd_hbm.1, s32[16]{0:T(128)} %sizes_hbm.1, s32[4,128]{1,0:T(4,128)} %bitcast.3, f32[16,128]{1,0:T(8,128)} %bitcast.2, f32[8]{0:T(128)} %energies_hbm.1), custom_call_target="tpu_custom_call" | custom-call | flops 2400000000 | bytes 5000000 | tf_op jit(solution)/shard_map/pallas_call | solution.py:277
  51.0 1.3 %copy.8 = f32[8,512,128]{2,1,0:T(8,128)} copy(f32[8,512,128]{2,1,0:T(8,128)S(1)} %shard_map.64) | data formatting | bytes 4194304
